TPU v7x, 512 devices: a whole 4x8x8 slice. The times are simulated.
512 devices in a mesh: row: 16 (over y, z_hi), col: 32 (over x, z_lo, core).
Axes of the slice: x: 4, y: 8, z: 8 (z_hi: 2, z_lo: 4; z = z_hi * 4 + z_lo), core: 2. Of those that a mesh axis runs over, the one named last changes fastest.
Arguments:
- factor: bfloat16 [28672, 28672], P('row', 'col'), may hold values from -2 to 2, as said below
- gradient: float32 [28672, 2048], P(('row', 'col')), may hold values from -6 to 6
- starts: int32 [16], replicated, may hold values from 0 to 15, each once
Outputs:
- solved: float32 [28672, 2048], P(('row', 'col'))
Inputs may be any that keep to these rules, and one draw needn't show every extreme that they name: `factor`: tiles above the block diagonal are zero, and every diagonal tile is upper triangular. `starts`: every block column is the start of exactly one panel.
All inputs are finite; a program needn't handle non-finite values.
Results may differ from a plain program's by a relative error of at most 0.0046.
Values may be sent and summed in bfloat16 or wider, within the bound.
A program may use at most 64 MiB of HBM per device.

v0:
```python
import jax
import jax.numpy as jnp
from jax import lax
from jax.sharding import PartitionSpec as P

TICKS = 6


def partner(array, axis, bit):
    return lax.ppermute(array, axis, [(i, i ^ 1 << bit) for i in range(lax.axis_size(axis))])


def broadcast(value, axis, source):
    kept = jnp.where(lax.axis_index(axis) == source, value, 0).astype(value.dtype)
    return lax.psum(kept, axis)


def shifted(block, axis, distance):
    devices = range(lax.axis_size(axis))
    route = [((i - distance) % len(devices), i) for i in devices]
    return lax.ppermute(block, axis, route)


def body(factor, gradient, starts):
    row_count = gradient.shape[0]
    block_count = starts.shape[0]
    panel_width = gradient.shape[1] // block_count
    tile_rows = factor.shape[0]
    half_rows = factor.shape[1]
    col_count = lax.axis_size("col")
    row_idx = lax.axis_index("row")
    col_idx = lax.axis_index("col")
    block_col = col_idx // 2
    half_idx = col_idx % 2
    slots = jnp.arange(block_count, dtype=jnp.int32)
    start_hot = (starts[None, :] == slots[:, None]).astype(jnp.float32)
    pieces = gradient.reshape(2, row_count // 2, block_count, panel_width)
    ordered = jnp.einsum("jp,hrpw->jhrw", start_hot, pieces, precision=lax.Precision.HIGHEST)
    ordered = ordered.reshape(col_count * (row_count // 2), panel_width)
    received = lax.all_to_all(ordered, "col", split_axis=0, concat_axis=0, tiled=True)
    received = received.reshape(col_count, row_count // 2, panel_width)
    keep_first = (half_idx == 0).astype(jnp.float32)
    keep_second = 1.0 - keep_first
    buffer = jnp.stack([received * keep_first, received * keep_second], axis=1).reshape(
        tile_rows, panel_width
    )
    zeros_tile = jnp.zeros((tile_rows, panel_width), jnp.float32)
    for tick_idx in range(TICKS):
        active = block_col >= tick_idx
        on_diag = active & (row_idx == block_col)
        below_diag = active & (row_idx > block_col)
        summed = buffer + partner(buffer, "col", 0)
        rounded = summed.astype(jnp.bfloat16)
        solution = lax.dot_general(
            factor, rounded, (((0,), (0,)), ((), ())), preferred_element_type=jnp.float32
        )
        solution_bf = solution.astype(jnp.bfloat16)
        arrived = broadcast(solution_bf, "row", block_col)
        update = jnp.dot(factor, arrived, preferred_element_type=jnp.float32)
        placed = lax.dynamic_update_slice_in_dim(zeros_tile, solution, half_idx * half_rows, 0)
        buffer = jnp.where(on_diag, placed, jnp.where(below_diag, buffer - update, buffer))
        if tick_idx + 1 < TICKS:
            buffer = shifted(buffer, "col", 2)
    end_hot = (((starts + (TICKS - 1)) % block_count)[None, :] == slots[:, None]).astype(
        jnp.float32
    )
    returned = lax.all_to_all(buffer, "col", split_axis=0, concat_axis=0, tiled=True)
    slot_rows = returned.reshape(block_count, 2, row_count, panel_width).sum(axis=1)
    result = jnp.einsum("jp,jrw->rpw", end_hot, slot_rows, precision=lax.Precision.HIGHEST)
    return result.reshape(row_count, block_count * panel_width)


def solution(mesh):
    in_specs = (P("row", "col"), P(("row", "col"), None), P())
    out_specs = P(("row", "col"), None)
    return jax.shard_map(body, mesh=mesh, in_specs=in_specs, out_specs=out_specs, check_vma=False)
```

profile of v0, /device:TPU:1, one launch (start us, length us, event | category | flops | bytes accessed | tf_op | source)
XLA Modules:
  0.0 1403.5 jit_solution(1890911971000149336)
XLA Ops:
  10.2 11.3 all-to-all-start
  21.6 16.8 %all-to-all-done = f32[32,28,128]{2,1,0:T(8,128)} async-done(((f32[32,28,128]{2,1,0:T(8,128)}), f32[32,28,128]{2,1,0:T(8,128)}, u32[]{:S(2)}, u32[]{:S(2)}) %all-to-all-start) | async-done | bytes 458784 | tf_op jit(solution)/shard_map/all_to_all | solution.py:40
  40.8 2.2 reshape.29
  43.0 2.0 collective-permute-start
  45.1 2.6 collective-permute-done
  48.7 2.9 constant_dynamic-update-slice_fusion.5
  52.5 2.4 copy.13
  54.9 185.7 %all-reduce.7.cloned.1.call-done = bf16[896,128]{0,1:T(8,128)(2,1)} async-done(((bf16[896,128]{0,1:T(8,128)(2,1)}), bf16[896,128]{0,1:T(8,128)(2,1)}) %all-reduce.7.cloned.1.call-update) | async-done | bytes 229392 | tf_op jit(solution)/shard_map/psum | solution.py:15
  240.6 2.6 fusion.17
  243.2 2.2 collective-permute-start.1
  245.4 15.9 %collective-permute-done.1 = f32[1792,128]{0,1:T(8,128)S(1)} collective-permute-done((f32[1792,128]{0,1:T(8,128)S(1)}, f32[1792,128]{0,1:T(8,128)S(1)}, u32[]{:S(2)}, u32[]{:S(2)}) %collective-permute-start.1) | collective-permute-done | bytes 917536 | tf_op jit(solution)/shard_map/ppermute | solution.py:21
  261.3 14.7 %collective-permute-start.2 = (f32[1792,128]{0,1:T(8,128)S(1)}, f32[1792,128]{0,1:T(8,128)S(1)}, u32[]{:S(2)}, u32[]{:S(2)}) collective-permute-start(f32[1792,128]{0,1:T(8,128)S(1)} %collective-permute-done.1), channel_id=1, source_target_pairs={{0,1},{1,0},{2,3},{3,2},{4,5},{5,4},{6,7},{7,6},{8,9},{9,8},{10,11... | collective-permute-start | bytes 2752520 | tf_op jit(solution)/shard_map/ppermute | solution.py:10
  275.9 2.1 collective-permute-done.2
  279.0 1.5 constant_dynamic-update-slice_fusion.4
  281.4 180.4 %all-reduce.9.cloned.1.call-done = bf16[896,128]{0,1:T(8,128)(2,1)} async-done(((bf16[896,128]{0,1:T(8,128)(2,1)}), bf16[896,128]{0,1:T(8,128)(2,1)}) %all-reduce.9.cloned.1.call-update) | async-done | bytes 229392 | tf_op jit(solution)/shard_map/psum | solution.py:15
  461.7 2.3 fusion.14
  464.1 2.5 collective-permute-start.3
  466.5 15.6 %collective-permute-done.3 = f32[1792,128]{0,1:T(8,128)S(1)} collective-permute-done((f32[1792,128]{0,1:T(8,128)S(1)}, f32[1792,128]{0,1:T(8,128)S(1)}, u32[]{:S(2)}, u32[]{:S(2)}) %collective-permute-start.3) | collective-permute-done | bytes 917536 | tf_op jit(solution)/shard_map/ppermute | solution.py:21
  482.2 14.7 %collective-permute-start.4 = (f32[1792,128]{0,1:T(8,128)S(1)}, f32[1792,128]{0,1:T(8,128)S(1)}, u32[]{:S(2)}, u32[]{:S(2)}) collective-permute-start(f32[1792,128]{0,1:T(8,128)S(1)} %collective-permute-done.3), channel_id=1, source_target_pairs={{0,1},{1,0},{2,3},{3,2},{4,5},{5,4},{6,7},{7,6},{8,9},{9,8},{10,11... | collective-permute-start | bytes 2752520 | tf_op jit(solution)/shard_map/ppermute | solution.py:10
  496.9 2.1 collective-permute-done.4
  499.9 1.5 constant_dynamic-update-slice_fusion.3
  502.3 180.6 %all-reduce.11.cloned.1.call-done = bf16[896,128]{0,1:T(8,128)(2,1)} async-done(((bf16[896,128]{0,1:T(8,128)(2,1)}), bf16[896,128]{0,1:T(8,128)(2,1)}) %all-reduce.11.cloned.1.call-update) | async-done | bytes 229392 | tf_op jit(solution)/shard_map/psum | solution.py:15
  682.9 2.3 fusion.11
  685.2 2.5 collective-permute-start.5
  687.7 15.6 %collective-permute-done.5 = f32[1792,128]{0,1:T(8,128)S(1)} collective-permute-done((f32[1792,128]{0,1:T(8,128)S(1)}, f32[1792,128]{0,1:T(8,128)S(1)}, u32[]{:S(2)}, u32[]{:S(2)}) %collective-permute-start.5) | collective-permute-done | bytes 917536 | tf_op jit(solution)/shard_map/ppermute | solution.py:21
  703.3 14.7 %collective-permute-start.6 = (f32[1792,128]{0,1:T(8,128)S(1)}, f32[1792,128]{0,1:T(8,128)S(1)}, u32[]{:S(2)}, u32[]{:S(2)}) collective-permute-start(f32[1792,128]{0,1:T(8,128)S(1)} %collective-permute-done.5), channel_id=1, source_target_pairs={{0,1},{1,0},{2,3},{3,2},{4,5},{5,4},{6,7},{7,6},{8,9},{9,8},{10,11... | collective-permute-start | bytes 2752520 | tf_op jit(solution)/shard_map/ppermute | solution.py:10
  718.0 2.1 collective-permute-done.6
  721.1 1.5 constant_dynamic-update-slice_fusion.2
  723.4 180.7 %all-reduce.13.cloned.1.call-done = bf16[896,128]{0,1:T(8,128)(2,1)} async-done(((bf16[896,128]{0,1:T(8,128)(2,1)}), bf16[896,128]{0,1:T(8,128)(2,1)}) %all-reduce.13.cloned.1.call-update) | async-done | bytes 229392 | tf_op jit(solution)/shard_map/psum | solution.py:15
  904.1 2.3 fusion.8
  906.4 2.5 collective-permute-start.7
  908.9 15.6 %collective-permute-done.7 = f32[1792,128]{0,1:T(8,128)S(1)} collective-permute-done((f32[1792,128]{0,1:T(8,128)S(1)}, f32[1792,128]{0,1:T(8,128)S(1)}, u32[]{:S(2)}, u32[]{:S(2)}) %collective-permute-start.7) | collective-permute-done | bytes 917536 | tf_op jit(solution)/shard_map/ppermute | solution.py:21
  924.5 14.7 %collective-permute-start.8 = (f32[1792,128]{0,1:T(8,128)S(1)}, f32[1792,128]{0,1:T(8,128)S(1)}, u32[]{:S(2)}, u32[]{:S(2)}) collective-permute-start(f32[1792,128]{0,1:T(8,128)S(1)} %collective-permute-done.7), channel_id=1, source_target_pairs={{0,1},{1,0},{2,3},{3,2},{4,5},{5,4},{6,7},{7,6},{8,9},{9,8},{10,11... | collective-permute-start | bytes 2752520 | tf_op jit(solution)/shard_map/ppermute | solution.py:10
  939.2 2.1 collective-permute-done.8
  942.3 1.5 constant_dynamic-update-slice_fusion.1
  944.6 180.7 %all-reduce.15.cloned.1.call-done = bf16[896,128]{0,1:T(8,128)(2,1)} async-done(((bf16[896,128]{0,1:T(8,128)(2,1)}), bf16[896,128]{0,1:T(8,128)(2,1)}) %all-reduce.15.cloned.1.call-update) | async-done | bytes 229392 | tf_op jit(solution)/shard_map/psum | solution.py:15
  1125.4 2.3 fusion.5
  1127.7 2.5 collective-permute-start.9
  1130.2 15.6 %collective-permute-done.9 = f32[1792,128]{0,1:T(8,128)S(1)} collective-permute-done((f32[1792,128]{0,1:T(8,128)S(1)}, f32[1792,128]{0,1:T(8,128)S(1)}, u32[]{:S(2)}, u32[]{:S(2)}) %collective-permute-start.9) | collective-permute-done | bytes 917536 | tf_op jit(solution)/shard_map/ppermute | solution.py:21
  1145.8 14.9 %collective-permute-start.10 = (f32[1792,128]{0,1:T(8,128)S(1)}, f32[1792,128]{0,1:T(8,128)S(1)}, u32[]{:S(2)}, u32[]{:S(2)}) collective-permute-start(f32[1792,128]{0,1:T(8,128)S(1)} %collective-permute-done.9), channel_id=1, source_target_pairs={{0,1},{1,0},{2,3},{3,2},{4,5},{5,4},{6,7},{7,6},{8,9},{9,8},{10,11... | collective-permute-start | bytes 2752520 | tf_op jit(solution)/shard_map/ppermute | solution.py:10
  1160.6 1.9 collective-permute-done.10
  1163.5 1.5 constant_dynamic-update-slice_fusion
  1165.8 180.7 %all-reduce.17.cloned.1.call-done = bf16[896,128]{0,1:T(8,128)(2,1)} async-done(((bf16[896,128]{0,1:T(8,128)(2,1)}), bf16[896,128]{0,1:T(8,128)(2,1)}) %all-reduce.17.cloned.1.call-update) | async-done | bytes 229392 | tf_op jit(solution)/shard_map/psum | solution.py:15
  1346.6 3.3 fusion.2
  1349.8 2.4 copy.15
  1352.3 16.6 %all-to-all-start.1 = ((f32[32,56,128]{2,1,0:T(8,128)}), f32[32,56,128]{2,1,0:T(8,128)}, u32[]{:S(2)}, u32[]{:S(2)}) async-start(f32[32,56,128]{2,1,0:T(8,128)} %bitcast.103), calls=%async_computation.1 | async-start | bytes 1835008 | tf_op jit(solution)/shard_map/all_to_all | solution.py:67
  1369.0 25.1 %all-to-all-done.1 = f32[32,56,128]{2,1,0:T(8,128)} async-done(((f32[32,56,128]{2,1,0:T(8,128)}), f32[32,56,128]{2,1,0:T(8,128)}, u32[]{:S(2)}, u32[]{:S(2)}) %all-to-all-start.1) | async-done | bytes 917536 | tf_op jit(solution)/shard_map/all_to_all | solution.py:67
  1394.1 1.3 bitcast_reduce_fusion
  (48 shorter events, 18.0 us)
Async XLA Ops:
  6.5 42.2 %copy-start = (bf16[1792,896]{1,0:T(8,128)(2,1)S(1)}, bf16[1792,896]{1,0:T(8,128)(2,1)}, u32[]{:S(2)}) copy-start(bf16[1792,896]{1,0:T(8,128)(2,1)} %param.3) | copy-start | bytes 9633796
  10.2 28.2 %all-to-all-start = ((f32[32,28,128]{2,1,0:T(8,128)}), f32[32,28,128]{2,1,0:T(8,128)}, u32[]{:S(2)}, u32[]{:S(2)}) async-start(f32[32,28,128]{2,1,0:T(8,128)} %copy.11), calls=%async_computation | async-start | bytes 1048576 | tf_op jit(solution)/shard_map/all_to_all | solution.py:40
  21.5 219.0 %all-reduce.7.cloned.1.call-start = ((), (), s32[]{:S(2)}) async-start(), calls=%async_computation.2 | async-start | bytes 458752 | tf_op jit(solution)/shard_map/psum | solution.py:15
  43.0 4.7 collective-permute-start
  52.4 409.4 %all-reduce.9.cloned.1.call-start = ((), (), s32[]{:S(2)}) async-start(), calls=%async_computation.3 | async-start | bytes 458752 | tf_op jit(solution)/shard_map/psum | solution.py:15
  243.2 18.1 %collective-permute-start.1 = (f32[1792,128]{0,1:T(8,128)S(1)}, f32[1792,128]{0,1:T(8,128)S(1)}, u32[]{:S(2)}, u32[]{:S(2)}) collective-permute-start(f32[1792,128]{0,1:T(8,128)S(1)} %fusion.17), channel_id=1, source_target_pairs={{30,0},{31,1},{0,2},{1,3},{2,4},{3,5},{4,6},{5,7},{6,8},{7,9},{8,1... | collective-permute-start | bytes 2752520 | tf_op jit(solution)/shard_map/ppermute | solution.py:21
  261.3 19.3 %copy-start.2 = (f32[1792,128]{0,1:T(8,128)}, f32[1792,128]{0,1:T(8,128)S(1)}, u32[]{:S(2)}) copy-start(f32[1792,128]{0,1:T(8,128)S(1)} %collective-permute-done.1) | copy-start | bytes 2752516
  261.3 16.8 %collective-permute-start.2 = (f32[1792,128]{0,1:T(8,128)S(1)}, f32[1792,128]{0,1:T(8,128)S(1)}, u32[]{:S(2)}, u32[]{:S(2)}) collective-permute-start(f32[1792,128]{0,1:T(8,128)S(1)} %collective-permute-done.1), channel_id=1, source_target_pairs={{0,1},{1,0},{2,3},{3,2},{4,5},{5,4},{6,7},{7,6},{8,9},{9,8},{10,11... | collective-permute-start | bytes 2752520 | tf_op jit(solution)/shard_map/ppermute | solution.py:10
  281.3 401.6 %all-reduce.11.cloned.1.call-start = ((), (), s32[]{:S(2)}) async-start(), calls=%async_computation.4 | async-start | bytes 458752 | tf_op jit(solution)/shard_map/psum | solution.py:15
  464.1 18.1 %collective-permute-start.3 = (f32[1792,128]{0,1:T(8,128)S(1)}, f32[1792,128]{0,1:T(8,128)S(1)}, u32[]{:S(2)}, u32[]{:S(2)}) collective-permute-start(f32[1792,128]{0,1:T(8,128)S(1)} %fusion.14), channel_id=1, source_target_pairs={{30,0},{31,1},{0,2},{1,3},{2,4},{3,5},{4,6},{5,7},{6,8},{7,9},{8,1... | collective-permute-start | bytes 2752520 | tf_op jit(solution)/shard_map/ppermute | solution.py:21
  482.2 19.3 %copy-start.3 = (f32[1792,128]{0,1:T(8,128)}, f32[1792,128]{0,1:T(8,128)S(1)}, u32[]{:S(2)}) copy-start(f32[1792,128]{0,1:T(8,128)S(1)} %collective-permute-done.3) | copy-start | bytes 2752516
  482.2 16.8 %collective-permute-start.4 = (f32[1792,128]{0,1:T(8,128)S(1)}, f32[1792,128]{0,1:T(8,128)S(1)}, u32[]{:S(2)}, u32[]{:S(2)}) collective-permute-start(f32[1792,128]{0,1:T(8,128)S(1)} %collective-permute-done.3), channel_id=1, source_target_pairs={{0,1},{1,0},{2,3},{3,2},{4,5},{5,4},{6,7},{7,6},{8,9},{9,8},{10,11... | collective-permute-start | bytes 2752520 | tf_op jit(solution)/shard_map/ppermute | solution.py:10
  502.2 401.9 %all-reduce.13.cloned.1.call-start = ((), (), s32[]{:S(2)}) async-start(), calls=%async_computation.5 | async-start | bytes 458752 | tf_op jit(solution)/shard_map/psum | solution.py:15
  685.2 18.1 %collective-permute-start.5 = (f32[1792,128]{0,1:T(8,128)S(1)}, f32[1792,128]{0,1:T(8,128)S(1)}, u32[]{:S(2)}, u32[]{:S(2)}) collective-permute-start(f32[1792,128]{0,1:T(8,128)S(1)} %fusion.11), channel_id=1, source_target_pairs={{30,0},{31,1},{0,2},{1,3},{2,4},{3,5},{4,6},{5,7},{6,8},{7,9},{8,1... | collective-permute-start | bytes 2752520 | tf_op jit(solution)/shard_map/ppermute | solution.py:21
  703.3 19.3 %copy-start.4 = (f32[1792,128]{0,1:T(8,128)}, f32[1792,128]{0,1:T(8,128)S(1)}, u32[]{:S(2)}) copy-start(f32[1792,128]{0,1:T(8,128)S(1)} %collective-permute-done.5) | copy-start | bytes 2752516
  703.3 16.8 %collective-permute-start.6 = (f32[1792,128]{0,1:T(8,128)S(1)}, f32[1792,128]{0,1:T(8,128)S(1)}, u32[]{:S(2)}, u32[]{:S(2)}) collective-permute-start(f32[1792,128]{0,1:T(8,128)S(1)} %collective-permute-done.5), channel_id=1, source_target_pairs={{0,1},{1,0},{2,3},{3,2},{4,5},{5,4},{6,7},{7,6},{8,9},{9,8},{10,11... | collective-permute-start | bytes 2752520 | tf_op jit(solution)/shard_map/ppermute | solution.py:10
  723.4 402.0 %all-reduce.15.cloned.1.call-start = ((), (), s32[]{:S(2)}) async-start(), calls=%async_computation.6 | async-start | bytes 458752 | tf_op jit(solution)/shard_map/psum | solution.py:15
  906.4 18.1 %collective-permute-start.7 = (f32[1792,128]{0,1:T(8,128)S(1)}, f32[1792,128]{0,1:T(8,128)S(1)}, u32[]{:S(2)}, u32[]{:S(2)}) collective-permute-start(f32[1792,128]{0,1:T(8,128)S(1)} %fusion.8), channel_id=1, source_target_pairs={{30,0},{31,1},{0,2},{1,3},{2,4},{3,5},{4,6},{5,7},{6,8},{7,9},{8,1... | collective-permute-start | bytes 2752520 | tf_op jit(solution)/shard_map/ppermute | solution.py:21
  924.5 19.3 %copy-start.5 = (f32[1792,128]{0,1:T(8,128)}, f32[1792,128]{0,1:T(8,128)S(1)}, u32[]{:S(2)}) copy-start(f32[1792,128]{0,1:T(8,128)S(1)} %collective-permute-done.7) | copy-start | bytes 2752516
  924.5 16.8 %collective-permute-start.8 = (f32[1792,128]{0,1:T(8,128)S(1)}, f32[1792,128]{0,1:T(8,128)S(1)}, u32[]{:S(2)}, u32[]{:S(2)}) collective-permute-start(f32[1792,128]{0,1:T(8,128)S(1)} %collective-permute-done.7), channel_id=1, source_target_pairs={{0,1},{1,0},{2,3},{3,2},{4,5},{5,4},{6,7},{7,6},{8,9},{9,8},{10,11... | collective-permute-start | bytes 2752520 | tf_op jit(solution)/shard_map/ppermute | solution.py:10
  944.6 402.0 %all-reduce.17.cloned.1.call-start = ((), (), s32[]{:S(2)}) async-start(), calls=%async_computation.7 | async-start | bytes 458752 | tf_op jit(solution)/shard_map/psum | solution.py:15
  1127.7 18.1 %collective-permute-start.9 = (f32[1792,128]{0,1:T(8,128)S(1)}, f32[1792,128]{0,1:T(8,128)S(1)}, u32[]{:S(2)}, u32[]{:S(2)}) collective-permute-start(f32[1792,128]{0,1:T(8,128)S(1)} %fusion.5), channel_id=1, source_target_pairs={{30,0},{31,1},{0,2},{1,3},{2,4},{3,5},{4,6},{5,7},{6,8},{7,9},{8,1... | collective-permute-start | bytes 2752520 | tf_op jit(solution)/shard_map/ppermute | solution.py:21
  1145.8 19.3 %copy-start.1 = (f32[1792,128]{0,1:T(8,128)}, f32[1792,128]{0,1:T(8,128)S(1)}, u32[]{:S(2)}) copy-start(f32[1792,128]{0,1:T(8,128)S(1)} %collective-permute-done.9) | copy-start | bytes 2752516
  1145.8 16.8 %collective-permute-start.10 = (f32[1792,128]{0,1:T(8,128)S(1)}, f32[1792,128]{0,1:T(8,128)S(1)}, u32[]{:S(2)}, u32[]{:S(2)}) collective-permute-start(f32[1792,128]{0,1:T(8,128)S(1)} %collective-permute-done.9), channel_id=1, source_target_pairs={{0,1},{1,0},{2,3},{3,2},{4,5},{5,4},{6,7},{7,6},{8,9},{9,8},{10,11... | collective-permute-start | bytes 2752520 | tf_op jit(solution)/shard_map/ppermute | solution.py:10
  1349.8 19.1 %copy-start.6 = (s32[16]{0:T(128)S(1)}, s32[16]{0:T(128)}, u32[]{:S(2)}) copy-start(s32[16]{0:T(128)} %param.5) | copy-start | bytes 196
  1352.3 41.8 %all-to-all-start.1 = ((f32[32,56,128]{2,1,0:T(8,128)}), f32[32,56,128]{2,1,0:T(8,128)}, u32[]{:S(2)}, u32[]{:S(2)}) async-start(f32[32,56,128]{2,1,0:T(8,128)} %bitcast.103), calls=%async_computation.1 | async-start | bytes 1835008 | tf_op jit(solution)/shard_map/all_to_all | solution.py:67
Sparse Core Ops, SparseCore 0:
  52.5 188.0 all-reduce.6
  281.4 180.2 all-reduce.8
  502.3 180.5 all-reduce.10
  723.5 180.5 all-reduce.12
  944.7 180.6 all-reduce.14
  1165.9 180.5 all-reduce.16
where the time goes:
time: 1400 us
  waiting for transfers between devices  1220 us (87%)
  starting transfers between devices  116 us (8%)
  matrix products  27.1 us (2%)
  local copies, waits for them, and re-layouts  17.9 us (1%)
    psum x6, waiting for transfers between devices, broadcast(): return lax.psum(kept, axis)  1090 us
    ppermute x5, waiting for transfers between devices, shifted(): return lax.ppermute(block, axis, route)  78.4 us
    ppermute x6, starting transfers between devices, partner(): lax.ppermute(array, axis, [(i, i ^ 1 << bit) for i in range(lax.axis_size...  75.6 us
  transfers between devices with their start and end apart: 19, of which 19 were waited for; matrix products, arithmetic and copies ran while one was open for 0% of the time, Pallas kernels for 0%

commit v1 on v0

--- a/solution.py
+++ b/solution.py
@@ -6,13 +6,19 @@
 TICKS = 6
 
 
+def gather_and_add(x, axis):
+    shards = lax.all_gather(x, axis, axis=0, tiled=False)
+    result = shards.sum(axis=0)
+    return result
+
+
 def partner(array, axis, bit):
     return lax.ppermute(array, axis, [(i, i ^ 1 << bit) for i in range(lax.axis_size(axis))])
 
 
 def broadcast(value, axis, source):
     kept = jnp.where(lax.axis_index(axis) == source, value, 0).astype(value.dtype)
-    return lax.psum(kept, axis)
+    return gather_and_add(kept, axis)
 
 
 def shifted(block, axis, distance):

time: 1400 us -> 1020 us (0.73)
  waiting for transfers between devices: 1220 us -> 867 us
  starting transfers between devices: 116 us -> 65.9 us
  local copies, waits for them, and re-layouts: 17.9 us -> 34.2 us
    psum x6 -> x0, waiting for transfers between devices: 1090 us -> none  [broadcast(): return lax.psum(kept, axis)]
    all_gather x0 -> x6, waiting for transfers between devices: none -> 703 us  [gather_and_add(): shards = lax.all_gather(x, axis, axis=0, tiled=False)]
    ppermute x6, starting transfers between devices: 75.6 us -> 35.2 us  [partner(): lax.ppermute(array, axis, [(i, i ^ 1 << bit) for i in range(lax.axis_size...]
    ppermute x5, waiting for transfers between devices: 78.4 us -> 110 us  [shifted(): return lax.ppermute(block, axis, route)]
    unnamed x16 -> x34, local copies, waits for them, and re-layouts: 2.19 us -> 18.5 us
where the time goes in v1:
time: 1020 us
  waiting for transfers between devices  867 us (85%)
  starting transfers between devices  65.9 us (6%)
  local copies, waits for them, and re-layouts  34.2 us (3%)
  matrix products  20 us (2%)
  other arithmetic  17.4 us (2%)
  between operations  14 us (1%)
    all_gather x6, waiting for transfers between devices, gather_and_add(): shards = lax.all_gather(x, axis, axis=0, tiled=False)  703 us
    ppermute x5, waiting for transfers between devices, shifted(): return lax.ppermute(block, axis, route)  110 us
    ppermute x6, starting transfers between devices, partner(): lax.ppermute(array, axis, [(i, i ^ 1 << bit) for i in range(lax.axis_size...  35.2 us
    all_to_all x1, waiting for transfers between devices, body(): lax.all_to_all(buffer, 'col', split_axis=0, concat_axis=0, tiled=True)  25.1 us
  transfers between devices with their start and end apart: 19, of which 19 were waited for; matrix products, arithmetic and copies ran while one was open for 0% of the time, Pallas kernels for 0%

profile of v1, /device:TPU:1, one launch (start us, length us, event | category | flops | bytes accessed | tf_op | source)
XLA Modules:
  0.0 1018.6 jit_solution(7055214598382885685)
XLA Ops:
  10.2 11.3 %all-to-all-start = ((f32[32,28,128]{2,1,0:T(8,128)}), f32[32,28,128]{2,1,0:T(8,128)}, u32[]{:S(2)}, u32[]{:S(2)}) async-start(f32[32,28,128]{2,1,0:T(8,128)} %copy.11), calls=%async_computation | async-start | bytes 1048576 | tf_op jit(solution)/shard_map/all_to_all | solution.py:46
  21.6 16.8 %all-to-all-done = f32[32,28,128]{2,1,0:T(8,128)} async-done(((f32[32,28,128]{2,1,0:T(8,128)}), f32[32,28,128]{2,1,0:T(8,128)}, u32[]{:S(2)}, u32[]{:S(2)}) %all-to-all-start) | async-done | bytes 458784 | tf_op jit(solution)/shard_map/all_to_all | solution.py:46
  40.7 2.2 reshape.29
  43.0 2.0 collective-permute-start
  45.0 2.6 collective-permute-done
  48.7 2.9 constant_dynamic-update-slice_fusion.5
  52.4 2.4 copy.13
  54.8 120.5 %all-gather.13.cloned.1.call-done = bf16[14336,128]{0,1:T(8,128)(2,1)} async-done(((bf16[896,128]{0,1:T(8,128)(2,1)}), bf16[14336,128]{0,1:T(8,128)(2,1)}) %all-gather.13.cloned.1.call-update) | async-done | bytes 3670032 | tf_op jit(solution)/shard_map/all_gather | solution.py:10
  175.4 2.7 copy.19
  178.1 1.8 bitcast_reduce_fusion.5
  179.9 2.2 fusion.17
  182.1 1.9 collective-permute-start.1
  184.0 21.9 %collective-permute-done.1 = f32[1792,128]{0,1:T(8,128)S(1)} collective-permute-done((f32[1792,128]{0,1:T(8,128)S(1)}, f32[1792,128]{0,1:T(8,128)S(1)}, u32[]{:S(2)}, u32[]{:S(2)}) %collective-permute-start.1) | collective-permute-done | bytes 917536 | tf_op jit(solution)/shard_map/ppermute | solution.py:27
  206.0 6.6 collective-permute-start.2
  212.6 2.1 collective-permute-done.2
  217.9 115.5 %all-gather.15.cloned.1.call-done = bf16[14336,128]{0,1:T(8,128)(2,1)} async-done(((bf16[896,128]{0,1:T(8,128)(2,1)}), bf16[14336,128]{0,1:T(8,128)(2,1)}) %all-gather.15.cloned.1.call-update) | async-done | bytes 3670032 | tf_op jit(solution)/shard_map/all_gather | solution.py:10
  333.4 2.7 copy.20
  336.2 1.8 bitcast_reduce_fusion.4
  339.0 1.9 collective-permute-start.3
  340.9 21.9 %collective-permute-done.3 = f32[1792,128]{0,1:T(8,128)S(1)} collective-permute-done((f32[1792,128]{0,1:T(8,128)S(1)}, f32[1792,128]{0,1:T(8,128)S(1)}, u32[]{:S(2)}, u32[]{:S(2)}) %collective-permute-start.3) | collective-permute-done | bytes 917536 | tf_op jit(solution)/shard_map/ppermute | solution.py:27
  362.9 6.6 collective-permute-start.4
  369.5 2.1 collective-permute-done.4
  375.0 116.5 %all-gather.17.cloned.1.call-done = bf16[14336,128]{0,1:T(8,128)(2,1)} async-done(((bf16[896,128]{0,1:T(8,128)(2,1)}), bf16[14336,128]{0,1:T(8,128)(2,1)}) %all-gather.17.cloned.1.call-update) | async-done | bytes 3670032 | tf_op jit(solution)/shard_map/all_gather | solution.py:10
  491.5 2.7 copy.21
  494.2 1.8 bitcast_reduce_fusion.3
  497.1 1.9 collective-permute-start.5
  499.0 21.9 %collective-permute-done.5 = f32[1792,128]{0,1:T(8,128)S(1)} collective-permute-done((f32[1792,128]{0,1:T(8,128)S(1)}, f32[1792,128]{0,1:T(8,128)S(1)}, u32[]{:S(2)}, u32[]{:S(2)}) %collective-permute-start.5) | collective-permute-done | bytes 917536 | tf_op jit(solution)/shard_map/ppermute | solution.py:27
  520.9 6.6 collective-permute-start.6
  527.5 2.1 collective-permute-done.6
  532.9 116.7 %all-gather.19.cloned.1.call-done = bf16[14336,128]{0,1:T(8,128)(2,1)} async-done(((bf16[896,128]{0,1:T(8,128)(2,1)}), bf16[14336,128]{0,1:T(8,128)(2,1)}) %all-gather.19.cloned.1.call-update) | async-done | bytes 3670032 | tf_op jit(solution)/shard_map/all_gather | solution.py:10
  649.6 2.7 copy.22
  652.3 1.8 bitcast_reduce_fusion.2
  655.1 1.9 collective-permute-start.7
  657.1 21.9 %collective-permute-done.7 = f32[1792,128]{0,1:T(8,128)S(1)} collective-permute-done((f32[1792,128]{0,1:T(8,128)S(1)}, f32[1792,128]{0,1:T(8,128)S(1)}, u32[]{:S(2)}, u32[]{:S(2)}) %collective-permute-start.7) | collective-permute-done | bytes 917536 | tf_op jit(solution)/shard_map/ppermute | solution.py:27
  679.0 6.6 collective-permute-start.8
  685.6 2.1 collective-permute-done.8
  691.0 116.7 %all-gather.21.cloned.1.call-done = bf16[14336,128]{0,1:T(8,128)(2,1)} async-done(((bf16[896,128]{0,1:T(8,128)(2,1)}), bf16[14336,128]{0,1:T(8,128)(2,1)}) %all-gather.21.cloned.1.call-update) | async-done | bytes 3670032 | tf_op jit(solution)/shard_map/all_gather | solution.py:10
  807.6 2.7 copy.23
  813.2 1.9 collective-permute-start.9
  815.1 21.9 %collective-permute-done.9 = f32[1792,128]{0,1:T(8,128)S(1)} collective-permute-done((f32[1792,128]{0,1:T(8,128)S(1)}, f32[1792,128]{0,1:T(8,128)S(1)}, u32[]{:S(2)}, u32[]{:S(2)}) %collective-permute-start.9) | collective-permute-done | bytes 917536 | tf_op jit(solution)/shard_map/ppermute | solution.py:27
  837.1 6.8 collective-permute-start.10
  843.9 1.9 collective-permute-done.10
  849.0 116.7 %all-gather.23.cloned.1.call-done = bf16[14336,128]{0,1:T(8,128)(2,1)} async-done(((bf16[896,128]{0,1:T(8,128)(2,1)}), bf16[14336,128]{0,1:T(8,128)(2,1)}) %all-gather.23.cloned.1.call-update) | async-done | bytes 3670032 | tf_op jit(solution)/shard_map/all_gather | solution.py:10
  965.7 2.7 copy.24
  970.2 2.0 fusion.2
  972.2 2.4 copy.15
  974.6 9.4 all-to-all-start.1
  984.1 25.1 %all-to-all-done.1 = f32[32,56,128]{2,1,0:T(8,128)} async-done(((f32[32,56,128]{2,1,0:T(8,128)}), f32[32,56,128]{2,1,0:T(8,128)}, u32[]{:S(2)}, u32[]{:S(2)}) %all-to-all-start.1) | async-done | bytes 917536 | tf_op jit(solution)/shard_map/all_to_all | solution.py:73
  (72 shorter events, 34.6 us)
Async XLA Ops:
  6.5 42.1 %copy-start = (bf16[1792,896]{1,0:T(8,128)(2,1)S(1)}, bf16[1792,896]{1,0:T(8,128)(2,1)}, u32[]{:S(2)}) copy-start(bf16[1792,896]{1,0:T(8,128)(2,1)} %param.3) | copy-start | bytes 9633796
  10.2 28.2 %all-to-all-start = ((f32[32,28,128]{2,1,0:T(8,128)}), f32[32,28,128]{2,1,0:T(8,128)}, u32[]{:S(2)}, u32[]{:S(2)}) async-start(f32[32,28,128]{2,1,0:T(8,128)} %copy.11), calls=%async_computation | async-start | bytes 1048576 | tf_op jit(solution)/shard_map/all_to_all | solution.py:46
  21.5 153.8 %all-gather.13.cloned.1.call-start = ((), (), s32[]{:S(2)}) async-start(), calls=%async_computation.2 | async-start | bytes 3899392 | tf_op jit(solution)/shard_map/all_gather | solution.py:10
  43.0 4.7 collective-permute-start
  52.3 281.1 %all-gather.15.cloned.1.call-start = ((), (), s32[]{:S(2)}) async-start(), calls=%async_computation.3 | async-start | bytes 3899392 | tf_op jit(solution)/shard_map/all_gather | solution.py:10
  178.1 1.8 copy-start.1
  182.1 23.9 %collective-permute-start.1 = (f32[1792,128]{0,1:T(8,128)S(1)}, f32[1792,128]{0,1:T(8,128)S(1)}, u32[]{:S(2)}, u32[]{:S(2)}) collective-permute-start(f32[1792,128]{0,1:T(8,128)S(1)} %fusion.17), channel_id=1, source_target_pairs={{30,0},{31,1},{0,2},{1,3},{2,4},{3,5},{4,6},{5,7},{6,8},{7,9},{8,1... | collective-permute-start | bytes 2752520 | tf_op jit(solution)/shard_map/ppermute | solution.py:27
  206.0 11.2 %copy-start.4 = (f32[1792,128]{0,1:T(8,128)}, f32[1792,128]{0,1:T(8,128)S(1)}, u32[]{:S(2)}) copy-start(f32[1792,128]{0,1:T(8,128)S(1)} %collective-permute-done.1) | copy-start | bytes 2752516
  206.0 8.7 collective-permute-start.2
  217.9 273.6 %all-gather.17.cloned.1.call-start = ((), (), s32[]{:S(2)}) async-start(), calls=%async_computation.4 | async-start | bytes 3899392 | tf_op jit(solution)/shard_map/all_gather | solution.py:10
  336.2 1.8 copy-start.5
  339.0 23.9 %collective-permute-start.3 = (f32[1792,128]{0,1:T(8,128)S(1)}, f32[1792,128]{0,1:T(8,128)S(1)}, u32[]{:S(2)}, u32[]{:S(2)}) collective-permute-start(f32[1792,128]{0,1:T(8,128)S(1)} %fusion.14), channel_id=1, source_target_pairs={{30,0},{31,1},{0,2},{1,3},{2,4},{3,5},{4,6},{5,7},{6,8},{7,9},{8,1... | collective-permute-start | bytes 2752520 | tf_op jit(solution)/shard_map/ppermute | solution.py:27
  362.9 11.2 %copy-start.6 = (f32[1792,128]{0,1:T(8,128)}, f32[1792,128]{0,1:T(8,128)S(1)}, u32[]{:S(2)}) copy-start(f32[1792,128]{0,1:T(8,128)S(1)} %collective-permute-done.3) | copy-start | bytes 2752516
  362.9 8.7 collective-permute-start.4
  374.8 274.8 %all-gather.19.cloned.1.call-start = ((), (), s32[]{:S(2)}) async-start(), calls=%async_computation.5 | async-start | bytes 3899392 | tf_op jit(solution)/shard_map/all_gather | solution.py:10
  494.2 1.8 copy-start.7
  497.1 23.9 %collective-permute-start.5 = (f32[1792,128]{0,1:T(8,128)S(1)}, f32[1792,128]{0,1:T(8,128)S(1)}, u32[]{:S(2)}, u32[]{:S(2)}) collective-permute-start(f32[1792,128]{0,1:T(8,128)S(1)} %fusion.11), channel_id=1, source_target_pairs={{30,0},{31,1},{0,2},{1,3},{2,4},{3,5},{4,6},{5,7},{6,8},{7,9},{8,1... | collective-permute-start | bytes 2752520 | tf_op jit(solution)/shard_map/ppermute | solution.py:27
  520.9 11.2 %copy-start.8 = (f32[1792,128]{0,1:T(8,128)}, f32[1792,128]{0,1:T(8,128)S(1)}, u32[]{:S(2)}) copy-start(f32[1792,128]{0,1:T(8,128)S(1)} %collective-permute-done.5) | copy-start | bytes 2752516
  520.9 8.7 collective-permute-start.6
  532.8 274.8 %all-gather.21.cloned.1.call-start = ((), (), s32[]{:S(2)}) async-start(), calls=%async_computation.6 | async-start | bytes 3899392 | tf_op jit(solution)/shard_map/all_gather | solution.py:10
  652.3 1.8 copy-start.9
  655.1 23.9 %collective-permute-start.7 = (f32[1792,128]{0,1:T(8,128)S(1)}, f32[1792,128]{0,1:T(8,128)S(1)}, u32[]{:S(2)}, u32[]{:S(2)}) collective-permute-start(f32[1792,128]{0,1:T(8,128)S(1)} %fusion.8), channel_id=1, source_target_pairs={{30,0},{31,1},{0,2},{1,3},{2,4},{3,5},{4,6},{5,7},{6,8},{7,9},{8,1... | collective-permute-start | bytes 2752520 | tf_op jit(solution)/shard_map/ppermute | solution.py:27
  679.0 11.2 %copy-start.10 = (f32[1792,128]{0,1:T(8,128)}, f32[1792,128]{0,1:T(8,128)S(1)}, u32[]{:S(2)}) copy-start(f32[1792,128]{0,1:T(8,128)S(1)} %collective-permute-done.7) | copy-start | bytes 2752516
  679.0 8.7 collective-permute-start.8
  690.9 274.8 %all-gather.23.cloned.1.call-start = ((), (), s32[]{:S(2)}) async-start(), calls=%async_computation.7 | async-start | bytes 3899392 | tf_op jit(solution)/shard_map/all_gather | solution.py:10
  810.4 1.8 copy-start.11
  813.2 23.9 %collective-permute-start.9 = (f32[1792,128]{0,1:T(8,128)S(1)}, f32[1792,128]{0,1:T(8,128)S(1)}, u32[]{:S(2)}, u32[]{:S(2)}) collective-permute-start(f32[1792,128]{0,1:T(8,128)S(1)} %fusion.5), channel_id=1, source_target_pairs={{30,0},{31,1},{0,2},{1,3},{2,4},{3,5},{4,6},{5,7},{6,8},{7,9},{8,1... | collective-permute-start | bytes 2752520 | tf_op jit(solution)/shard_map/ppermute | solution.py:27
  837.1 11.2 %copy-start.2 = (f32[1792,128]{0,1:T(8,128)}, f32[1792,128]{0,1:T(8,128)S(1)}, u32[]{:S(2)}) copy-start(f32[1792,128]{0,1:T(8,128)S(1)} %collective-permute-done.9) | copy-start | bytes 2752516
  837.1 8.7 collective-permute-start.10
  968.4 1.8 copy-start.3
  972.2 11.9 %copy-start.12 = (s32[16]{0:T(128)S(1)}, s32[16]{0:T(128)}, u32[]{:S(2)}) copy-start(s32[16]{0:T(128)} %param.5) | copy-start | bytes 196
  974.6 34.6 %all-to-all-start.1 = ((f32[32,56,128]{2,1,0:T(8,128)}), f32[32,56,128]{2,1,0:T(8,128)}, u32[]{:S(2)}, u32[]{:S(2)}) async-start(f32[32,56,128]{2,1,0:T(8,128)} %bitcast.139), calls=%async_computation.1 | async-start | bytes 1835008 | tf_op jit(solution)/shard_map/all_to_all | solution.py:73
Sparse Core Ops, SparseCore 0:
  52.5 122.8 all-gather.12
  218.0 115.3 all-gather.14
  374.9 116.5 all-gather.16
  533.0 116.5 all-gather.18
  691.0 116.5 all-gather.20
  849.1 116.5 all-gather.22
